TPU v7x, 32 devices: a whole 2x2x4 slice. The times are simulated.
32 devices in a mesh: xy: 8 (over z, x), gz: 4 (over y, core).
Axes of the slice: x: 2, y: 2, z: 4, core: 2. Of those that a mesh axis runs over, the one named last changes fastest.
Arguments:
- observed: float32 [256, 128, 256], P('gz', 'xy'), may hold values from 0.5 to 18
- estimate: float32 [256, 128, 256], P('gz', 'xy'), may hold values from 0.5 to 8
- lateral_psf: float32 [9, 9], replicated, may hold values from 0.0075 to 1.03
- depth_psf: float32 [64], replicated, may hold values from 0.0075 to 1.03
Outputs:
- restored: float32 [256, 128, 256], P('gz', 'xy')
All inputs are finite; a program needn't handle non-finite values.
Results may differ from a plain program's by a relative error of at most 0.0001.
Values sent between devices are 32-bit elements; how exact they have to be, the bound alone decides.
A program may use at most 64 MiB of HBM per device.

v0:
```python
import jax
import jax.numpy as jnp
from jax import lax
from jax.sharding import PartitionSpec as P

KZ = 64
ITERS = 2


def extended(cells, sides, width):
    for axis, dim in sides:
        count = lax.axis_size(axis)
        ends = count - 1
        head = lax.slice_in_dim(cells, 0, width, axis=dim)
        tail = lax.slice_in_dim(cells, cells.shape[dim] - width, cells.shape[dim], axis=dim)
        cells = jnp.concatenate(
            [
                lax.ppermute(tail, axis, [(i, (i + 1) % count) for i in range(ends)]),
                cells,
                lax.ppermute(head, axis, [((i + 1) % count, i) for i in range(ends)]),
            ],
            axis=dim,
        )
    return cells


def lateral(volume, kernel):
    taps_count = kernel.shape[0]
    reach = taps_count // 2
    padded = extended(volume, (("xy", 1),), reach)
    padded = jnp.pad(padded, ((0, 0), (0, 0), (reach, reach)))
    rows_out = volume.shape[1]
    cols_out = volume.shape[2]
    result = jnp.zeros(volume.shape, jnp.float32)
    for shift_a in range(taps_count):
        for shift_b in range(taps_count):
            result = (
                result
                + kernel[shift_a, shift_b]
                * padded[:, shift_a : shift_a + rows_out, shift_b : shift_b + cols_out]
            )
    return result


def depth_band(volume, depth_taps, offset):
    block = 128
    taps_count = depth_taps.shape[0]
    blocked = volume.reshape(volume.shape[0] // block, block, -1)
    offset_k = jnp.arange(3, dtype=jnp.int32)[:, None, None] - 1
    rows_in = jnp.arange(block, dtype=jnp.int32)[None, :, None]
    cols_out = jnp.arange(block, dtype=jnp.int32)[None, None, :]
    position = offset_k * block + rows_in - cols_out + offset
    onehot = (position[..., None] == jnp.arange(taps_count, dtype=jnp.int32)).astype(
        depth_taps.dtype
    )
    tables = jnp.einsum("kijt,t->kij", onehot, depth_taps, precision=lax.Precision.HIGHEST)
    partial_sums = jnp.einsum("kij,bic->kbjc", tables, blocked, precision=lax.Precision.HIGHEST)
    empty_block = jnp.zeros_like(partial_sums[0, :1])
    result = (
        partial_sums[1]
        + jnp.concatenate([partial_sums[2, 1:], empty_block], 0)
        + jnp.concatenate([empty_block, partial_sums[0, :-1]], 0)
    )
    return result.reshape(volume.shape)


def to_pencils(volume):
    return lax.all_to_all(volume, "gz", split_axis=1, concat_axis=0, tiled=True)


def from_pencils(volume):
    return lax.all_to_all(volume, "gz", split_axis=0, concat_axis=1, tiled=True)


def body(observed, estimate, lateral_psf, depth_psf):
    lateral_norm = lateral_psf / jnp.sum(lateral_psf)
    depth_norm = depth_psf / jnp.sum(depth_psf)
    lateral_flip = lateral_norm[::-1, ::-1]
    depth_flip = depth_norm[::-1]
    offset = KZ // 2
    offset_flip = KZ - 1 - offset
    current = estimate
    for repeat in range(ITERS):
        blurred = from_pencils(
            depth_band(to_pencils(lateral(current, lateral_norm)), depth_norm, offset)
        )
        quotient = observed / blurred
        correction = lateral(
            from_pencils(depth_band(to_pencils(quotient), depth_flip, offset_flip)), lateral_flip
        )
        current = current * correction
    return current


def solution(mesh):
    return jax.shard_map(
        body,
        mesh=mesh,
        in_specs=(P("gz", "xy", None), P("gz", "xy", None), P(), P()),
        out_specs=P("gz", "xy", None),
        check_vma=False,
    )
```

profile of v0, /device:TPU:17, one launch (start us, length us, event | category | flops | bytes accessed | tf_op | source)
XLA Modules:
  0.0 533.6 jit_solution(13350124785201483702)
XLA Ops:
  23.1 71.9 %fusion.297 = f32[64,16,256]{2,0,1:T(8,128)} fusion(f32[64,24,264]{2,0,1:T(8,128)S(1)} %select_maximum_fusion.6, f32[64,20,256]{2,0,1:T(8,128)} %constant_dynamic-update-slice_fusion.2, f32[64,20,256]{2,0,1:T(8,128)} %copy-done.1, f32[]{:T(128)} %bitcast.81, f32[]{:T(128)} %bitcast.80, f32[]{:T(128)} %bitcast.79, f32[]{:T(128)} %bitcast.78, f32[]{:T(128)} %bitcast.77, ...), kind=kLoop, calls=%fused_computation.576 | loop fusion | flops 42205184 | bytes 85983552 | tf_op jit(solution)/shard_map/add | solution.py:38
  95.0 4.9 all-to-all-start
  100.1 4.5 fusion
  104.6 8.8 %all-to-all-done = f32[64,16,256]{2,0,1:T(8,128)S(1)} async-done(((f32[64,16,256]{2,0,1:T(8,128)}), f32[64,16,256]{2,0,1:T(8,128)S(1)}, u32[]{:S(2)}, u32[]{:S(2)}) %all-to-all-start) | async-done | bytes 1048608 | tf_op jit(solution)/shard_map/all_to_all | solution.py:68
  118.4 16.7 %all_to_all.132 = f32[256,4,256]{2,1,0:T(4,128)S(1)} all-to-all(f32[256,4,256]{2,1,0:T(4,128)S(1)} %reshape.66), channel_id=1, replica_groups=mesh['xy'=8,'gz'=4] {'gz'}, dimensions={0} | all-to-all | bytes 2097152 | tf_op jit(solution)/shard_map/all_to_all | solution.py:72
  137.9 4.9 all-to-all-start.2
  143.0 4.5 fusion.1
  147.5 8.9 %all-to-all-done.2 = f32[64,16,256]{2,0,1:T(8,128)S(1)} async-done(((f32[64,16,256]{2,0,1:T(8,128)}), f32[64,16,256]{2,0,1:T(8,128)S(1)}, u32[]{:S(2)}, u32[]{:S(2)}) %all-to-all-start.2) | async-done | bytes 1048608 | tf_op jit(solution)/shard_map/all_to_all | solution.py:68
  162.3 4.4 all-to-all-start.3
  168.2 12.1 %all-to-all-done.3 = f32[256,4,256]{2,1,0:T(4,128)S(1)} async-done(((f32[256,4,256]{2,1,0:T(4,128)}), f32[256,4,256]{2,1,0:T(4,128)S(1)}, u32[]{:S(2)}, u32[]{:S(2)}) %all-to-all-start.3) | async-done | bytes 1048608 | tf_op jit(solution)/shard_map/all_to_all | solution.py:72
  180.7 4.1 collective-permute-start.2
  189.0 6.1 %collective-permute-done.2 = f32[64,4,256]{2,0,1:T(8,128)S(1)} collective-permute-done((f32[64,4,256]{2,0,1:T(8,128)S(1)}, f32[64,4,256]{2,0,1:T(8,128)S(1)}, u32[]{:S(2)}, u32[]{:S(2)}) %collective-permute-start.2) | collective-permute-done | bytes 262176 | tf_op jit(solution)/shard_map/ppermute | solution.py:18
  198.0 72.0 %fusion.190 = f32[64,16,256]{2,0,1:T(8,128)S(1)} fusion(f32[64,16,256]{2,0,1:T(8,128)} %bitcast.305, f32[64,4,256]{2,0,1:T(8,128)} %copy-done.13, f32[64,24,264]{2,0,1:T(8,128)S(1)} %select_maximum_fusion.4, f32[64,4,256]{2,0,1:T(8,128)} %copy-done.12, f32[]{:T(128)} %bitcast.191, f32[]{:T(128)} %bitcast.190, f32[]{:T(128)} %bitcast.189, f32[]{:T(128)} %bitcast.188, ...), kind=kLoop, calls=%fused_computation.242 | loop fusion | flops 44564480 | bytes 79167808 | tf_op jit(solution)/shard_map/mul | solution.py:91
  272.0 4.3 collective-permute-start.5
  276.4 3.8 collective-permute-done.4
  280.2 6.4 %collective-permute-done.5 = f32[64,4,256]{2,0,1:T(8,128)S(1)} collective-permute-done((f32[64,4,256]{2,0,1:T(8,128)S(1)}, f32[64,4,256]{2,0,1:T(8,128)S(1)}, u32[]{:S(2)}, u32[]{:S(2)}) %collective-permute-start.5) | collective-permute-done | bytes 262176 | tf_op jit(solution)/shard_map/ppermute | solution.py:20
  288.1 71.3 %fusion.105 = f32[64,16,256]{2,0,1:T(8,128)} fusion(f32[64,16,256]{2,0,1:T(8,128)S(1)} %fusion.190, f32[64,4,256]{2,0,1:T(8,128)} %copy-done.11, f32[64,24,264]{2,0,1:T(8,128)S(1)} %select_maximum_fusion.2, f32[64,4,256]{2,0,1:T(8,128)} %copy-done.9, f32[]{:T(128)} %bitcast.81, f32[]{:T(128)} %bitcast.80, f32[]{:T(128)} %bitcast.79, f32[]{:T(128)} %bitcast.78, ...), kind=kLoop, calls=%fused_computation.157 | loop fusion | flops 44302336 | bytes 78119232 | tf_op jit(solution)/shard_map/add | solution.py:38
  359.4 17.4 %all_to_all.133 = f32[64,16,256]{2,0,1:T(8,128)S(1)} all-to-all(f32[64,16,256]{2,0,1:T(8,128)} %fusion.105), channel_id=1, replica_groups=mesh['xy'=8,'gz'=4] {'gz'}, dimensions={1} | all-to-all | bytes 2097152 | tf_op jit(solution)/shard_map/all_to_all | solution.py:68
  381.7 17.1 %all_to_all.134 = f32[256,4,256]{2,1,0:T(4,128)S(1)} all-to-all(f32[256,4,256]{2,1,0:T(4,128)S(1)} %reshape.70), channel_id=1, replica_groups=mesh['xy'=8,'gz'=4] {'gz'}, dimensions={0} | all-to-all | bytes 2097152 | tf_op jit(solution)/shard_map/all_to_all | solution.py:72
  400.7 16.9 %all_to_all.135 = f32[64,16,256]{2,0,1:T(8,128)S(1)} all-to-all(f32[64,16,256]{2,0,1:T(8,128)S(1)} %bitcast_divide_fusion), channel_id=1, replica_groups=mesh['xy'=8,'gz'=4] {'gz'}, dimensions={1} | all-to-all | bytes 2097152 | tf_op jit(solution)/shard_map/all_to_all | solution.py:68
  422.6 16.9 %all_to_all.136 = f32[256,4,256]{2,1,0:T(4,128)S(1)} all-to-all(f32[256,4,256]{2,1,0:T(4,128)S(1)} %reshape.72), channel_id=1, replica_groups=mesh['xy'=8,'gz'=4] {'gz'}, dimensions={0} | all-to-all | bytes 2097152 | tf_op jit(solution)/shard_map/all_to_all | solution.py:72
  441.7 4.5 collective-permute-start.7
  449.4 7.0 %collective-permute-done.7 = f32[64,4,256]{2,0,1:T(8,128)S(1)} collective-permute-done((f32[64,4,256]{2,0,1:T(8,128)S(1)}, f32[64,4,256]{2,0,1:T(8,128)S(1)}, u32[]{:S(2)}, u32[]{:S(2)}) %collective-permute-start.7) | collective-permute-done | bytes 262176 | tf_op jit(solution)/shard_map/ppermute | solution.py:20
  457.8 72.7 %fusion.21 = f32[64,16,256]{2,0,1:T(8,128)} fusion(f32[64,16,256]{2,0,1:T(8,128)S(1)} %fusion.190, f32[64,16,256]{2,0,1:T(8,128)} %bitcast.302, f32[64,4,256]{2,0,1:T(8,128)} %copy-done.10, f32[64,24,264]{2,0,1:T(8,128)S(1)} %select_maximum_fusion, f32[64,4,256]{2,0,1:T(8,128)} %copy-done.8, f32[]{:T(128)} %bitcast.191, f32[]{:T(128)} %bitcast.190, ...), kind=kLoop, calls=%fused_computation.73 | loop fusion | flops 44564480 | bytes 79167808 | tf_op jit(solution)/shard_map/mul | solution.py:91
  (120 shorter events, 70.3 us)
Async XLA Ops:
  0.0 14.8 %copy-start = (f32[64,16,256]{2,1,0:T(8,128)S(1)}, f32[64,16,256]{2,1,0:T(8,128)}, u32[]{:S(2)}) copy-start(f32[64,16,256]{2,1,0:T(8,128)} %param.5) | copy-start | bytes 3145732
  0.0 9.2 %copy-start.19 = (f32[9,9]{1,0:T(8,128)S(1)}, f32[9,9]{1,0:T(8,128)}, u32[]{:S(2)}) copy-start(f32[9,9]{1,0:T(8,128)} %param.6) | copy-start | bytes 976
  0.0 12.7 %copy-start.20 = (f32[64]{0:T(128)S(1)}, f32[64]{0:T(128)}, u32[]{:S(2)}) copy-start(f32[64]{0:T(128)} %param.7) | copy-start | bytes 772
  3.0 11.8 %collective-permute-start = (f32[64,4,256]{2,0,1:T(8,128)S(1)}, f32[64,4,256]{2,0,1:T(8,128)S(1)}, u32[]{:S(2)}, u32[]{:S(2)}) collective-permute-start(f32[64,4,256]{2,0,1:T(8,128)S(1)} %get-tuple-element.21), channel_id=1, source_target_pairs={{0,4},{4,8},{8,12},{12,16},{16,20},{20,24},{24,28},{1,5},{5,9},{9,... | collective-permute-start | bytes 786440 | tf_op jit(solution)/shard_map/ppermute | solution.py:18
  6.1 13.6 %collective-permute-start.1 = (f32[64,4,256]{2,0,1:T(8,128)S(1)}, f32[64,4,256]{2,0,1:T(8,128)}, u32[]{:S(2)}, u32[]{:S(2)}) collective-permute-start(f32[64,4,256]{2,0,1:T(8,128)S(1)} %get-tuple-element.22), channel_id=1, source_target_pairs={{4,0},{8,4},{12,8},{16,12},{20,16},{24,20},{28,24},{5,1},{9,5},{13... | collective-permute-start | bytes 786440 | tf_op jit(solution)/shard_map/ppermute | solution.py:20
  13.3 6.4 %copy-start.5 = (f32[64,16,256]{2,0,1:T(8,128)S(1)}, f32[64,16,256]{2,0,1:T(8,128)}, u32[]{:S(2)}) copy-start(f32[64,16,256]{2,0,1:T(8,128)} %copy-done.4) | copy-start | bytes 3145732
  14.7 1.7 copy-start.14
  95.0 18.4 %all-to-all-start = ((f32[64,16,256]{2,0,1:T(8,128)}), f32[64,16,256]{2,0,1:T(8,128)S(1)}, u32[]{:S(2)}, u32[]{:S(2)}) async-start(f32[64,16,256]{2,0,1:T(8,128)} %fusion.297), calls=%async_computation | async-start | bytes 2097152 | tf_op jit(solution)/shard_map/all_to_all | solution.py:68
  104.6 12.8 %copy-start.15 = (f32[1,3,128,128]{3,0,2,1:T(1,128)}, f32[1,3,128,128]{3,0,2,1:T(1,128)S(1)}, u32[]{:S(2)}) copy-start(f32[1,3,128,128]{3,0,2,1:T(1,128)S(1)} %fusion) | copy-start | bytes 589828
  137.9 18.5 %all-to-all-start.2 = ((f32[64,16,256]{2,0,1:T(8,128)}), f32[64,16,256]{2,0,1:T(8,128)S(1)}, u32[]{:S(2)}, u32[]{:S(2)}) async-start(f32[64,16,256]{2,0,1:T(8,128)} %bitcast_divide_fusion.1), calls=%async_computation.2 | async-start | bytes 2097152 | tf_op jit(solution)/shard_map/all_to_all | solution.py:68
  147.5 12.9 %copy-start.17 = (f32[1,3,128,128]{3,0,2,1:T(1,128)}, f32[1,3,128,128]{3,0,2,1:T(1,128)S(1)}, u32[]{:S(2)}) copy-start(f32[1,3,128,128]{3,0,2,1:T(1,128)S(1)} %fusion.1) | copy-start | bytes 589828
  162.3 18.0 %all-to-all-start.3 = ((f32[256,4,256]{2,1,0:T(4,128)}), f32[256,4,256]{2,1,0:T(4,128)S(1)}, u32[]{:S(2)}, u32[]{:S(2)}) async-start(f32[256,4,256]{2,1,0:T(4,128)} %reshape.68), calls=%async_computation.3 | async-start | bytes 2097152 | tf_op jit(solution)/shard_map/all_to_all | solution.py:72
  180.6 17.4 %copy-start.3 = (f32[64,4,4,256]{3,0,2,1:T(8,128)}, f32[64,4,4,256]{3,0,2,1:T(8,128)S(1)}, u32[]{:S(2)}) copy-start(f32[64,4,4,256]{3,0,2,1:T(8,128)S(1)} %copy.133) | copy-start | bytes 3145732
  180.7 14.5 %collective-permute-start.2 = (f32[64,4,256]{2,0,1:T(8,128)S(1)}, f32[64,4,256]{2,0,1:T(8,128)S(1)}, u32[]{:S(2)}, u32[]{:S(2)}) collective-permute-start(f32[64,4,256]{2,0,1:T(8,128)S(1)} %get-tuple-element.17), channel_id=1, source_target_pairs={{0,4},{4,8},{8,12},{12,16},{16,20},{20,24},{24,28},{1,5},{5,9},{9,... | collective-permute-start | bytes 786440 | tf_op jit(solution)/shard_map/ppermute | solution.py:18
  184.8 12.5 %collective-permute-start.3 = (f32[64,4,256]{2,0,1:T(8,128)S(1)}, f32[64,4,256]{2,0,1:T(8,128)S(1)}, u32[]{:S(2)}, u32[]{:S(2)}) collective-permute-start(f32[64,4,256]{2,0,1:T(8,128)S(1)} %get-tuple-element.18), channel_id=1, source_target_pairs={{4,0},{8,4},{12,8},{16,12},{20,16},{24,20},{28,24},{5,1},{9,5},{13... | collective-permute-start | bytes 786440 | tf_op jit(solution)/shard_map/ppermute | solution.py:20
  195.1 2.9 copy-start.12
  270.0 10.2 %collective-permute-start.4 = (f32[64,4,256]{2,0,1:T(8,128)S(1)}, f32[64,4,256]{2,0,1:T(8,128)S(1)}, u32[]{:S(2)}, u32[]{:S(2)}) collective-permute-start(f32[64,4,256]{2,0,1:T(8,128)S(1)} %get-tuple-element.15), channel_id=1, source_target_pairs={{0,4},{4,8},{8,12},{12,16},{16,20},{20,24},{24,28},{1,5},{5,9},{9,... | collective-permute-start | bytes 786440 | tf_op jit(solution)/shard_map/ppermute | solution.py:18
  272.0 14.6 %collective-permute-start.5 = (f32[64,4,256]{2,0,1:T(8,128)S(1)}, f32[64,4,256]{2,0,1:T(8,128)S(1)}, u32[]{:S(2)}, u32[]{:S(2)}) collective-permute-start(f32[64,4,256]{2,0,1:T(8,128)S(1)} %get-tuple-element.16), channel_id=1, source_target_pairs={{4,0},{8,4},{12,8},{16,12},{20,16},{24,20},{28,24},{5,1},{9,5},{13... | collective-permute-start | bytes 786440 | tf_op jit(solution)/shard_map/ppermute | solution.py:20
  280.2 6.4 %copy-start.9 = (f32[64,4,256]{2,0,1:T(8,128)}, f32[64,4,256]{2,0,1:T(8,128)S(1)}, u32[]{:S(2)}) copy-start(f32[64,4,256]{2,0,1:T(8,128)S(1)} %collective-permute-done.4) | copy-start | bytes 786436
  376.8 1.2 copy-start.16
  439.7 16.7 %copy-start.2 = (f32[64,4,4,256]{3,0,2,1:T(8,128)}, f32[64,4,4,256]{3,0,2,1:T(8,128)S(1)}, u32[]{:S(2)}) copy-start(f32[64,4,4,256]{3,0,2,1:T(8,128)S(1)} %copy.149) | copy-start | bytes 3145732
  439.8 9.6 %collective-permute-start.6 = (f32[64,4,256]{2,0,1:T(8,128)S(1)}, f32[64,4,256]{2,0,1:T(8,128)S(1)}, u32[]{:S(2)}, u32[]{:S(2)}) collective-permute-start(f32[64,4,256]{2,0,1:T(8,128)S(1)} %get-tuple-element.13), channel_id=1, source_target_pairs={{0,4},{4,8},{8,12},{12,16},{16,20},{20,24},{24,28},{1,5},{5,9},{9,... | collective-permute-start | bytes 786440 | tf_op jit(solution)/shard_map/ppermute | solution.py:18
  441.7 14.7 %collective-permute-start.7 = (f32[64,4,256]{2,0,1:T(8,128)S(1)}, f32[64,4,256]{2,0,1:T(8,128)S(1)}, u32[]{:S(2)}, u32[]{:S(2)}) collective-permute-start(f32[64,4,256]{2,0,1:T(8,128)S(1)} %get-tuple-element.14), channel_id=1, source_target_pairs={{4,0},{8,4},{12,8},{16,12},{20,16},{24,20},{28,24},{5,1},{9,5},{13... | collective-permute-start | bytes 786440 | tf_op jit(solution)/shard_map/ppermute | solution.py:20
  449.4 7.0 %copy-start.8 = (f32[64,4,256]{2,0,1:T(8,128)}, f32[64,4,256]{2,0,1:T(8,128)S(1)}, u32[]{:S(2)}) copy-start(f32[64,4,256]{2,0,1:T(8,128)S(1)} %collective-permute-done.6) | copy-start | bytes 786436
  (8 other events, 7.8 us)
where the time goes:
time: 543 us; the launch traced here: 534 us
  other arithmetic  296 us (55%)
  blocking collectives  85 us (16%)
  waiting for transfers between devices  60.9 us (11%)
  starting transfers between devices  39.3 us (7%)
  local copies, waits for them, and re-layouts  31.3 us (6%)
  matrix products  19.7 us (4%)
    mul x2, other arithmetic, body(): current = current * correction  145 us
    add x2, other arithmetic, lateral(): result + kernel[shift_a, shift_b] * padded[:, shift_a:shift_a + rows_out,...  143 us
    all_to_all x3, blocking collectives, from_pencils(): return lax.all_to_all(volume, 'gz', split_axis=0, concat_axis=1, tiled=True)  50.7 us
    all_to_all x2, blocking collectives, to_pencils(): return lax.all_to_all(volume, 'gz', split_axis=1, concat_axis=0, tiled=True)  34.3 us
    ppermute x4, waiting for transfers between devices, extended(): lax.ppermute(head, axis, [((i + 1) % count, i) for i in range(ends)])  17.9 us
    all_to_all x2, waiting for transfers between devices, to_pencils(): return lax.all_to_all(volume, 'gz', split_axis=1, concat_axis=0, tiled=True)  17.8 us
    ppermute x4, starting transfers between devices, extended(): lax.ppermute(head, axis, [((i + 1) % count, i) for i in range(ends)])  14 us
    ppermute x4, waiting for transfers between devices, extended(): lax.ppermute(tail, axis, [(i, (i + 1) % count) for i in range(ends)])  13.1 us
  transfers between devices with their start and end apart: 11, of which 10 were waited for; matrix products, arithmetic and copies ran while one was open for 4% of the time, Pallas kernels for 0%

commit v1 on v0

v1 whole, which is shorter than its diff:
```python
import functools

import jax
import jax.numpy as jnp
from jax import lax
from jax.experimental import pallas as pl
from jax.experimental.pallas import tpu as pltpu
from jax.sharding import PartitionSpec as P

ITERS = 2
CHUNKS = 4
MESH = pl.DeviceIdType.MESH
F32 = jnp.float32
BF16 = jnp.bfloat16


def split(value):
    high = value.astype(BF16)
    low = (value - high.astype(F32)).astype(BF16)
    return high, low


def total_of(ref, shape):
    total = None
    if len(shape) == 1:
        for i in range(shape[0]):
            total = ref[i] if total is None else total + ref[i]
    else:
        for i in range(shape[0]):
            for j in range(shape[1]):
                total = ref[i, j] if total is None else total + ref[i, j]
    return total


def lateral_tables(psf, total, tables, flip):
    taps = psf.shape[0]
    reach = taps // 2
    cols = tables.shape[2]
    block = 64
    inverse = 1.0 / jnp.full((1, cols), total, F32)

    def step(a, carry):
        for start in range(0, cols, block):
            rows_in = lax.broadcasted_iota(jnp.int32, (block, cols), 0) + start
            cols_out = lax.broadcasted_iota(jnp.int32, (block, cols), 1)
            offset = rows_in - cols_out + reach
            band = jnp.zeros((block, cols), F32)
            for b in range(taps):
                tap = psf[taps - 1 - a, taps - 1 - b] if flip else psf[a, b]
                band = jnp.where(offset == b, tap, band)
            high, low = split(band * inverse)
            tables[a, start : start + block, :] = high
            tables[a, cols + start : cols + start + block, :] = high
            tables[a, 2 * cols + start : 2 * cols + start + block, :] = low
        return carry

    lax.fori_loop(0, taps, step, 0)


def depth_tables(psf, total, table, slot, flip):
    taps = psf.shape[0]
    planes = table.shape[1] // 2
    width = table.shape[2] // 2
    rows = lax.broadcasted_iota(jnp.int32, (planes, width), 0)
    cols = lax.broadcasted_iota(jnp.int32, (planes, width), 1)
    tap_index = rows + taps - cols if flip else cols - rows
    band = jnp.zeros((planes, width), F32)
    for t in range(taps):
        band = jnp.where(tap_index == t, psf[t], band)
    high, low = split(band * (1.0 / jnp.full((1, width), total, F32)))
    table[slot] = jnp.concatenate(
        [
            jnp.concatenate([high, high], 1),
            jnp.concatenate([low, jnp.zeros_like(low)], 1),
        ],
        0,
    )


def kernel(
    nx, ng, obs_hbm, est_hbm, lat_psf, dep_psf, out,
    u0, u1, obs, v, q, w, xr, zr, ext_hi, ext_lo, lat_t, dep_t,
    in_sem, xs, xrs, vs, vrs, qs, qrs,
):
    rows, planes, cols = u0.shape
    reach = xr.shape[2]
    half = zr.shape[3]
    chunk = planes // CHUNKS
    xi = lax.axis_index("xy")
    gi = lax.axis_index("gz")
    has_left, has_right = xi > 0, xi < nx - 1
    has_prev, has_next = gi > 0, gi < ng - 1

    def order():
        edge = [0, rows - reach]
        return edge + [s for s in range(0, rows, reach) if s not in edge]

    est_in = {}
    obs_in = {}
    for s in order():
        for x in range(s, s + reach):
            est_in[x] = pltpu.make_async_copy(est_hbm.at[:, x, :], u0.at[x], in_sem.at[0, x])
            est_in[x].start()
    for x in range(rows):
        obs_in[x] = pltpu.make_async_copy(obs_hbm.at[:, x, :], obs.at[x], in_sem.at[1, x])
        obs_in[x].start()

    barrier = pltpu.get_barrier_semaphore()
    for there, axis, index in (
        (has_left, "xy", xi - 1), (has_right, "xy", xi + 1),
        (has_prev, "gz", gi - 1), (has_next, "gz", gi + 1),
    ):
        @pl.when(there)
        def _():
            pl.semaphore_signal(barrier, inc=1, device_id={axis: index}, device_id_type=MESH)

    for there, side in ((has_left, 0), (has_right, 1)):
        @pl.when(jnp.logical_not(there))
        def _():
            for p in range(2 * ITERS):
                xr[p, side] = jnp.zeros(xr.shape[2:], F32)

    for there, side in ((has_prev, 0), (has_next, 1)):
        @pl.when(jnp.logical_not(there))
        def _():
            for p in range(2 * ITERS):
                zr[p, side] = jnp.zeros(zr.shape[2:], F32)

    pl.semaphore_wait(
        barrier,
        has_left.astype(jnp.int32) + has_right.astype(jnp.int32)
        + has_prev.astype(jnp.int32) + has_next.astype(jnp.int32),
    )

    sent = []

    def x_copy(src, p, to_right, c):
        first = rows - reach if to_right else 0
        side = 0 if to_right else 1
        at = pl.ds(c * chunk, chunk)
        return pltpu.make_async_remote_copy(
            src_ref=src.at[pl.ds(first, reach), at, :],
            dst_ref=xr.at[p, side, :, at, :],
            send_sem=xs.at[p, side, c],
            recv_sem=xrs.at[p, side, c],
            device_id={"xy": xi + 1 if to_right else xi - 1},
            device_id_type=MESH,
        )

    def x_send(src, p, to_right, c):
        there = has_right if to_right else has_left
        copy = x_copy(src, p, to_right, c)
        sent.append((there, copy))

        @pl.when(there)
        def _():
            copy.start()

    def x_wait(src, p, c):
        for to_right, there in ((True, has_left), (False, has_right)):
            @pl.when(there)
            def _():
                x_copy(src, p, to_right, c).wait_recv()

    def v_copy(p, c):
        first = c * chunk
        to_next = first >= half
        landing = first - half if to_next else first
        return pltpu.make_async_remote_copy(
            src_ref=v.at[p, :, pl.ds(first, chunk), :],
            dst_ref=zr.at[2 * p, 0 if to_next else 1, :, pl.ds(landing, chunk), :],
            send_sem=vs.at[p, c],
            recv_sem=vrs.at[p, c],
            device_id={"gz": gi + 1 if to_next else gi - 1},
            device_id_type=MESH,
        )

    def v_send(p, c):
        there = has_next if c * chunk >= half else has_prev
        copy = v_copy(p, c)
        sent.append((there, copy))

        @pl.when(there)
        def _():
            copy.start()

    def v_wait(p):
        for c in range(CHUNKS):
            @pl.when(has_prev if c * chunk >= half else has_next)
            def _():
                v_copy(p, c).wait_recv()

    def q_copy(p, start, to_next):
        group = pl.ds(start, reach)
        side = 0 if to_next else 1
        return pltpu.make_async_remote_copy(
            src_ref=q.at[p, group, pl.ds(half if to_next else 0, half), :],
            dst_ref=zr.at[2 * p + 1, side, group, :, :],
            send_sem=qs.at[p, side, start // reach],
            recv_sem=qrs.at[p, side, start // reach],
            device_id={"gz": gi + 1 if to_next else gi - 1},
            device_id_type=MESH,
        )

    def q_send(p, start):
        for to_next, there in ((True, has_next), (False, has_prev)):
            copy = q_copy(p, start, to_next)
            sent.append((there, copy))

            @pl.when(there)
            def _():
                copy.start()

    def q_wait(p, start):
        for to_next, there in ((True, has_prev), (False, has_next)):
            @pl.when(there)
            def _():
                q_copy(p, start, to_next).wait_recv()

    def lateral(src, p, c, flip):
        at = pl.ds(c * chunk, chunk)
        slot = c % 2
        for piece, first, count in (
            (xr.at[p, 0], 0, reach), (src, reach, rows), (xr.at[p, 1], reach + rows, reach),
        ):
            high, low = split(piece[:, at, :])
            ext_hi[slot, first : first + count] = high
            ext_lo[slot, first : first + count] = low
        total = None
        for a in range(lat_t.shape[1]):
            high = ext_hi[slot, a : a + rows].reshape(rows * chunk, cols)
            low = ext_lo[slot, a : a + rows].reshape(rows * chunk, cols)
            part = jnp.dot(
                jnp.concatenate([high, low, high], 1), lat_t[flip, a], preferred_element_type=F32
            )
            total = part if total is None else total + part
        return total.reshape(rows, chunk, cols)

    def depth(src, p, x, flip):
        high, low = split(jnp.concatenate([zr[p, 0, x], src[x], zr[p, 1, x]], 0))
        both = jnp.dot(
            dep_t[flip], jnp.concatenate([high, low], 0), preferred_element_type=F32
        )
        return both[:planes] + both[planes:]

    for s in order()[:2]:
        for x in range(s, s + reach):
            est_in[x].wait()
        for c in range(CHUNKS):
            x_send(u0, 0, s > 0, c)

    lat_total = total_of(lat_psf, lat_psf.shape)
    dep_total = total_of(dep_psf, dep_psf.shape)
    for flip in (0, 1):
        lateral_tables(lat_psf, lat_total, lat_t.at[flip], flip)
        depth_tables(dep_psf, dep_total, dep_t, flip, flip)
    for s in order()[2:]:
        for x in range(s, s + reach):
            est_in[x].wait()
    for x in range(rows):
        obs_in[x].wait()

    current = u0
    for p in range(ITERS):
        for c in range(CHUNKS):
            x_wait(current, 2 * p, c)
            v[p, :, c * chunk : (c + 1) * chunk, :] = lateral(current, 2 * p, c, 0)
            v_send(p, c)
        v_wait(p)
        for s in order():
            for x in range(s, s + reach):
                q[p, x] = obs[x] / depth(v.at[p], 2 * p, x, 0)
            q_send(p, s)
        for s in order():
            q_wait(p, s)
            for x in range(s, s + reach):
                w[p, x] = depth(q.at[p], 2 * p + 1, x, 1)
            if s == 0 or s == rows - reach:
                for c in range(CHUNKS):
                    x_send(w.at[p], 2 * p + 1, s > 0, c)
        target = out if p == ITERS - 1 else u1
        for c in range(CHUNKS):
            at = slice(c * chunk, (c + 1) * chunk)
            x_wait(w.at[p], 2 * p + 1, c)
            target[:, at, :] = current[:, at, :] * lateral(w.at[p], 2 * p + 1, c, 1)
            if p < ITERS - 1:
                x_send(u1, 2 * p + 2, False, c)
                x_send(u1, 2 * p + 2, True, c)
        current = target

    for there, copy in sent:
        @pl.when(there)
        def _():
            copy.wait_send()


def body(nx, ng, observed, estimate, lateral_psf, depth_psf):
    planes, rows, cols = estimate.shape
    taps = lateral_psf.shape[0]
    reach = taps // 2
    half = depth_psf.shape[0] // 2
    chunk = planes // CHUNKS
    groups = rows // reach
    volume = (rows, planes, cols)
    dma = pltpu.SemaphoreType.DMA
    result = pl.pallas_call(
        functools.partial(kernel, nx, ng),
        out_shape=jax.ShapeDtypeStruct(volume, F32),
        in_specs=[
            pl.BlockSpec(memory_space=pl.ANY),
            pl.BlockSpec(memory_space=pl.ANY),
            pl.BlockSpec(memory_space=pltpu.SMEM),
            pl.BlockSpec(memory_space=pltpu.SMEM),
        ],
        out_specs=pl.BlockSpec(memory_space=pltpu.VMEM),
        scratch_shapes=[
            pltpu.VMEM(volume, F32),
            pltpu.VMEM(volume, F32),
            pltpu.VMEM(volume, F32),
            pltpu.VMEM((ITERS,) + volume, F32),
            pltpu.VMEM((ITERS,) + volume, F32),
            pltpu.VMEM((ITERS,) + volume, F32),
            pltpu.VMEM((2 * ITERS, 2, reach, planes, cols), F32),
            pltpu.VMEM((2 * ITERS, 2, rows, half, cols), F32),
            pltpu.VMEM((2, rows + 2 * reach, chunk, cols), BF16),
            pltpu.VMEM((2, rows + 2 * reach, chunk, cols), BF16),
            pltpu.VMEM((2, taps, 3 * cols, cols), BF16),
            pltpu.VMEM((2, 2 * planes, 2 * (planes + 2 * half)), BF16),
            dma((2, rows)),
            dma((2 * ITERS, 2, CHUNKS)),
            dma((2 * ITERS, 2, CHUNKS)),
            dma((ITERS, CHUNKS)),
            dma((ITERS, CHUNKS)),
            dma((ITERS, 2, groups)),
            dma((ITERS, 2, groups)),
        ],
        compiler_params=pltpu.CompilerParams(
            collective_id=0, has_side_effects=True, vmem_limit_bytes=48 * 1024 * 1024
        ),
        cost_estimate=pl.CostEstimate(
            flops=2 * 2 * ITERS * 3 * taps * planes * rows * cols * cols,
            bytes_accessed=3 * 4 * planes * rows * cols,
            transcendentals=0,
        ),
    )(observed, estimate, lateral_psf, depth_psf)
    return jnp.swapaxes(result, 0, 1)


def solution(mesh):
    return jax.shard_map(
        functools.partial(body, mesh.shape["xy"], mesh.shape["gz"]),
        mesh=mesh,
        in_specs=(P("gz", "xy", None), P("gz", "xy", None), P(), P()),
        out_specs=P("gz", "xy", None),
        check_vma=False,
    )
```

time: 543 us -> 87.7 us (0.16); the launches traced: 534 us -> 87.5 us
  other arithmetic: 296 us -> 0 us
  blocking collectives: 85 us -> 0 us
  Pallas kernels: 0 us -> 82.1 us
  waiting for transfers between devices: 60.9 us -> 0 us
  starting transfers between devices: 39.3 us -> 0 us
  local copies, waits for them, and re-layouts: 31.3 us -> 5.38 us
  matrix products: 19.7 us -> 0 us
    mul x3 -> x0, other arithmetic: 145 us -> none  [the longest x2 145 us: body(): current = current * correction]
    add x8 -> x0, other arithmetic: 144 us -> none  [the longest x2 143 us: lateral(): result + kernel[shift_a, shift_b] * padded[:, shift_a:shift_a + rows_out,...]
    all_to_all x5 -> x0, blocking collectives: 85 us -> none  [the longest x3 50.7 us: from_pencils(): return lax.all_to_all(volume, 'gz', split_axis=0, concat_axis=1, tiled=True)]
    pallas_call x0 -> x1, Pallas kernels: none -> 82.1 us  [body(): pl.pallas_call(functools.partial(kernel, nx, ng), out_shape=jax.ShapeDtyp...]
    ppermute x8 -> x0, waiting for transfers between devices: 31 us -> none  [the longest x4 17.9 us: extended(): lax.ppermute(head, axis, [((i + 1) % count, i) for i in range(ends)])]
    all_to_all x3 -> x0, waiting for transfers between devices: 29.9 us -> none  [the longest x2 17.8 us: to_pencils(): return lax.all_to_all(volume, 'gz', split_axis=1, concat_axis=0, tiled=True)]
    ppermute x8 -> x0, starting transfers between devices: 25.2 us -> none  [the longest x4 14 us: extended(): lax.ppermute(head, axis, [((i + 1) % count, i) for i in range(ends)])]
    dot_general x6 -> x0, matrix products: 19.7 us -> none  [the longest x4 10.7 us: depth_band(): jnp.einsum('kij,bic->kbjc', tables, blocked, precision=lax.Precision.HIGH...]
  transfers between devices with their start and end apart: 11 -> 0, of which waited for: 10 -> 0; matrix products, arithmetic and copies ran while one was open for 4% -> 0% of each run, Pallas kernels for 0% -> 0%
where the time goes in v1:
time: 87.7 us; the launch traced here: 87.5 us
  Pallas kernels  82.1 us (94%)
  local copies, waits for them, and re-layouts  5.38 us (6%)
    pallas_call x1, Pallas kernels, body(): pl.pallas_call(functools.partial(kernel, nx, ng), out_shape=jax.ShapeDtyp...  82.1 us
    unnamed x8, local copies, waits for them, and re-layouts  3.8 us

profile of v1, /device:TPU:17, one launch (start us, length us, event | category | flops | bytes accessed | tf_op | source)
XLA Modules:
  0.0 87.5 jit_solution(11660571941199230241)
XLA Ops:
  0.0 0.0 copy-start
  0.0 1.2 %copy-done = f32[64,16,256]{2,1,0:T(8,128)S(1)} copy-done((f32[64,16,256]{2,1,0:T(8,128)S(1)}, f32[64,16,256]{2,1,0:T(8,128)}, u32[]{:S(2)}) %copy-start) | copy-done | bytes 1048600
  1.2 0.0 copy-start.1
  1.2 1.2 %copy-done.1 = f32[64,16,256]{2,1,0:T(8,128)S(1)} copy-done((f32[64,16,256]{2,1,0:T(8,128)S(1)}, f32[64,16,256]{2,1,0:T(8,128)}, u32[]{:S(2)}) %copy-start.1) | copy-done | bytes 1048600
  2.5 0.0 copy-start.2
  2.5 0.7 copy-done.2
  3.1 0.0 copy-start.3
  3.2 0.7 copy-done.3
  3.8 82.1 %shard_map.46 = f32[16,64,256]{2,1,0:T(8,128)S(1)} custom-call(f32[64,16,256]{2,1,0:T(8,128)S(1)} %copy-done, f32[64,16,256]{2,1,0:T(8,128)S(1)} %copy-done.1, f32[9,9]{1,0:T(8,128)S(1)} %copy-done.2, f32[64]{0:T(128)S(1)} %copy-done.3), custom_call_target="tpu_custom_call" | custom-call | flops 14495514624 | bytes 3145728 | tf_op jit(solution)/shard_map/pallas_call | solution.py:306
  85.9 1.6 %copy.5 = f32[64,16,256]{2,1,0:T(8,128)} copy(f32[64,16,256]{2,0,1:T(8,128)S(1)} %bitcast.1) | data formatting | bytes 2097152 | tf_op jit(solution)/shard_map/transpose | solution.py:346
Async XLA Ops:
  0.0 1.2 %copy-start = (f32[64,16,256]{2,1,0:T(8,128)S(1)}, f32[64,16,256]{2,1,0:T(8,128)}, u32[]{:S(2)}) copy-start(f32[64,16,256]{2,1,0:T(8,128)} %obs_hbm.1) | copy-start | bytes 3145732
  1.2 1.2 %copy-start.1 = (f32[64,16,256]{2,1,0:T(8,128)S(1)}, f32[64,16,256]{2,1,0:T(8,128)}, u32[]{:S(2)}) copy-start(f32[64,16,256]{2,1,0:T(8,128)} %est_hbm.1) | copy-start | bytes 3145732
  2.5 0.7 copy-start.2
  3.1 0.7 copy-start.3

commit v2 on v1

--- a/solution.py
+++ b/solution.py
@@ -78,9 +78,9 @@
 
 
 def kernel(
-    nx, ng, obs_hbm, est_hbm, lat_psf, dep_psf, out,
+    nx, ng, obs_hbm, est_hbm, lat_hbm, dep_hbm, out,
     u0, u1, obs, v, q, w, xr, zr, ext_hi, ext_lo, lat_t, dep_t,
-    in_sem, xs, xrs, vs, vrs, qs, qrs,
+    lat_psf, dep_psf, in_sem, psf_sem, xs, xrs, vs, vrs, qs, qrs,
 ):
     rows, planes, cols = u0.shape
     reach = xr.shape[2]
@@ -101,6 +101,10 @@
         for x in range(s, s + reach):
             est_in[x] = pltpu.make_async_copy(est_hbm.at[:, x, :], u0.at[x], in_sem.at[0, x])
             est_in[x].start()
+    lat_in = pltpu.make_async_copy(lat_hbm, lat_psf, psf_sem.at[0])
+    dep_in = pltpu.make_async_copy(dep_hbm, dep_psf, psf_sem.at[1])
+    lat_in.start()
+    dep_in.start()
     for x in range(rows):
         obs_in[x] = pltpu.make_async_copy(obs_hbm.at[:, x, :], obs.at[x], in_sem.at[1, x])
         obs_in[x].start()
@@ -162,33 +166,34 @@
             def _():
                 x_copy(src, p, to_right, c).wait_recv()
 
-    def v_copy(p, c):
+    def v_copy(p, c, start):
         first = c * chunk
         to_next = first >= half
         landing = first - half if to_next else first
         return pltpu.make_async_remote_copy(
-            src_ref=v.at[p, :, pl.ds(first, chunk), :],
-            dst_ref=zr.at[2 * p, 0 if to_next else 1, :, pl.ds(landing, chunk), :],
-            send_sem=vs.at[p, c],
-            recv_sem=vrs.at[p, c],
+            src_ref=v.at[p, pl.ds(start, reach), pl.ds(first, chunk), :],
+            dst_ref=zr.at[2 * p, 0 if to_next else 1, pl.ds(start, reach), pl.ds(landing, chunk), :],
+            send_sem=vs.at[p, c, start // reach],
+            recv_sem=vrs.at[p, c, start // reach],
             device_id={"gz": gi + 1 if to_next else gi - 1},
             device_id_type=MESH,
         )
 
     def v_send(p, c):
         there = has_next if c * chunk >= half else has_prev
-        copy = v_copy(p, c)
-        sent.append((there, copy))
-
-        @pl.when(there)
-        def _():
-            copy.start()
-
-    def v_wait(p):
+        for start in order():
+            copy = v_copy(p, c, start)
+            sent.append((there, copy))
+
+            @pl.when(there)
+            def _():
+                copy.start()
+
+    def v_wait(p, start):
         for c in range(CHUNKS):
             @pl.when(has_prev if c * chunk >= half else has_next)
             def _():
-                v_copy(p, c).wait_recv()
+                v_copy(p, c, start).wait_recv()
 
     def q_copy(p, start, to_next):
         group = pl.ds(start, reach)
@@ -249,6 +254,8 @@
         for c in range(CHUNKS):
             x_send(u0, 0, s > 0, c)
 
+    lat_in.wait()
+    dep_in.wait()
     lat_total = total_of(lat_psf, lat_psf.shape)
     dep_total = total_of(dep_psf, dep_psf.shape)
     for flip in (0, 1):
@@ -257,8 +264,6 @@
     for s in order()[2:]:
         for x in range(s, s + reach):
             est_in[x].wait()
-    for x in range(rows):
-        obs_in[x].wait()
 
     current = u0
     for p in range(ITERS):
@@ -266,18 +271,31 @@
             x_wait(current, 2 * p, c)
             v[p, :, c * chunk : (c + 1) * chunk, :] = lateral(current, 2 * p, c, 0)
             v_send(p, c)
-        v_wait(p)
-        for s in order():
+        def forward(s):
+            v_wait(p, s)
             for x in range(s, s + reach):
+                if p == 0:
+                    obs_in[x].wait()
                 q[p, x] = obs[x] / depth(v.at[p], 2 * p, x, 0)
             q_send(p, s)
-        for s in order():
+
+        def backward(s):
             q_wait(p, s)
             for x in range(s, s + reach):
                 w[p, x] = depth(q.at[p], 2 * p + 1, x, 1)
             if s == 0 or s == rows - reach:
                 for c in range(CHUNKS):
                     x_send(w.at[p], 2 * p + 1, s > 0, c)
+
+        groups = order()
+        for s in groups[:3]:
+            forward(s)
+        for s in groups[:2]:
+            backward(s)
+        for s in groups[3:]:
+            forward(s)
+        for s in groups[2:]:
+            backward(s)
         target = out if p == ITERS - 1 else u1
         for c in range(CHUNKS):
             at = slice(c * chunk, (c + 1) * chunk)
@@ -307,10 +325,10 @@
         functools.partial(kernel, nx, ng),
         out_shape=jax.ShapeDtypeStruct(volume, F32),
         in_specs=[
-            pl.BlockSpec(memory_space=pl.ANY),
-            pl.BlockSpec(memory_space=pl.ANY),
-            pl.BlockSpec(memory_space=pltpu.SMEM),
-            pl.BlockSpec(memory_space=pltpu.SMEM),
+            pl.BlockSpec(memory_space=pltpu.HBM),
+            pl.BlockSpec(memory_space=pltpu.HBM),
+            pl.BlockSpec(memory_space=pltpu.HBM),
+            pl.BlockSpec(memory_space=pltpu.HBM),
         ],
         out_specs=pl.BlockSpec(memory_space=pltpu.VMEM),
         scratch_shapes=[
@@ -326,16 +344,19 @@
             pltpu.VMEM((2, rows + 2 * reach, chunk, cols), BF16),
             pltpu.VMEM((2, taps, 3 * cols, cols), BF16),
             pltpu.VMEM((2, 2 * planes, 2 * (planes + 2 * half)), BF16),
+            pltpu.SMEM(lateral_psf.shape, F32),
+            pltpu.SMEM(depth_psf.shape, F32),
             dma((2, rows)),
+            dma((2,)),
             dma((2 * ITERS, 2, CHUNKS)),
             dma((2 * ITERS, 2, CHUNKS)),
-            dma((ITERS, CHUNKS)),
-            dma((ITERS, CHUNKS)),
+            dma((ITERS, CHUNKS, groups)),
+            dma((ITERS, CHUNKS, groups)),
             dma((ITERS, 2, groups)),
             dma((ITERS, 2, groups)),
         ],
         compiler_params=pltpu.CompilerParams(
-            collective_id=0, has_side_effects=True, vmem_limit_bytes=48 * 1024 * 1024
+            collective_id=0, has_side_effects=True, vmem_limit_bytes=63 * 1024 * 1024
         ),
         cost_estimate=pl.CostEstimate(
             flops=2 * 2 * ITERS * 3 * taps * planes * rows * cols * cols,

time: 87.7 us -> 81 us (0.924)
  Pallas kernels: 82.1 us -> 78.1 us
  local copies, waits for them, and re-layouts: 5.38 us -> 2.81 us
    pallas_call x1, Pallas kernels: 82.1 us -> 78.1 us  [body(): pl.pallas_call(functools.partial(kernel, nx, ng), out_shape=jax.ShapeDtyp...]
    unnamed x8 -> x0, local copies, waits for them, and re-layouts: 3.8 us -> none
    transpose x1, local copies, waits for them, and re-layouts: 1.58 us -> 2.81 us  [body(): return jnp.swapaxes(result, 0, 1)]
where the time goes in v2:
time: 81 us; the launch traced here: 80.9 us
  Pallas kernels  78.1 us (96%)
  local copies, waits for them, and re-layouts  2.81 us (3%)
    pallas_call x1, Pallas kernels, body(): pl.pallas_call(functools.partial(kernel, nx, ng), out_shape=jax.ShapeDtyp...  78.1 us
    transpose x1, local copies, waits for them, and re-layouts, body(): return jnp.swapaxes(result, 0, 1)  2.81 us

profile of v2, /device:TPU:17, one launch (start us, length us, event | category | flops | bytes accessed | tf_op | source)
XLA Modules:
  0.0 80.9 jit_solution(13100382162351336372)
XLA Ops:
  0.0 78.1 %shard_map.46 = f32[16,64,256]{2,1,0:T(8,128)} custom-call(f32[64,16,256]{2,1,0:T(8,128)} %obs_hbm.1, f32[64,16,256]{2,1,0:T(8,128)} %est_hbm.1, f32[9,9]{1,0:T(8,128)} %lat_hbm.1, f32[64]{0:T(128)} %dep_hbm.1), custom_call_target="tpu_custom_call" | custom-call | flops 14495514624 | bytes 3145728 | tf_op jit(solution)/shard_map/pallas_call | solution.py:324
  78.1 2.8 %copy.5 = f32[64,16,256]{2,1,0:T(8,128)} copy(f32[64,16,256]{2,0,1:T(8,128)} %bitcast.1) | data formatting | bytes 2097152 | tf_op jit(solution)/shard_map/transpose | solution.py:367

commit v3 on v2

--- a/solution.py
+++ b/solution.py
@@ -179,9 +179,9 @@
             device_id_type=MESH,
         )
 
-    def v_send(p, c):
+    def v_send(p, c, starts):
         there = has_next if c * chunk >= half else has_prev
-        for start in order():
+        for start in starts:
             copy = v_copy(p, c, start)
             sent.append((there, copy))
 
@@ -222,24 +222,44 @@
             def _():
                 q_copy(p, start, to_next).wait_recv()
 
-    def lateral(src, p, c, flip):
-        at = pl.ds(c * chunk, chunk)
-        slot = c % 2
-        for piece, first, count in (
-            (xr.at[p, 0], 0, reach), (src, reach, rows), (xr.at[p, 1], reach + rows, reach),
-        ):
-            high, low = split(piece[:, at, :])
-            ext_hi[slot, first : first + count] = high
-            ext_lo[slot, first : first + count] = low
+    def place(value, c, first, count):
+        high, low = split(value)
+        ext_hi[c, first : first + count] = high
+        ext_lo[c, first : first + count] = low
+
+    def blur(flip, spans, slots):
         total = None
         for a in range(lat_t.shape[1]):
-            high = ext_hi[slot, a : a + rows].reshape(rows * chunk, cols)
-            low = ext_lo[slot, a : a + rows].reshape(rows * chunk, cols)
+            parts = []
+            for ext in (ext_hi, ext_lo):
+                pieces = [
+                    ext[c, first + a : first + a + count].reshape(count * chunk, cols)
+                    for c in slots
+                    for first, count in spans
+                ]
+                parts.append(pieces[0] if len(pieces) == 1 else jnp.concatenate(pieces, 0))
             part = jnp.dot(
-                jnp.concatenate([high, low, high], 1), lat_t[flip, a], preferred_element_type=F32
+                jnp.concatenate([parts[0], parts[1], parts[0]], 1),
+                lat_t[flip, a],
+                preferred_element_type=F32,
             )
             total = part if total is None else total + part
-        return total.reshape(rows, chunk, cols)
+        return total
+
+    inner = rows - 2 * reach
+
+    def blur_inner(src, slots, flip):
+        for c in slots:
+            place(src[:, c * chunk : (c + 1) * chunk, :], c, reach, rows)
+        total = blur(flip, [(reach, inner)], slots)
+        return total.reshape(len(slots), inner, chunk, cols)
+
+    def blur_edges(p, c, flip):
+        at = slice(c * chunk, (c + 1) * chunk)
+        place(xr[p, 0, :, at, :], c, 0, reach)
+        place(xr[p, 1, :, at, :], c, reach + rows, reach)
+        total = blur(flip, [(0, reach), (rows - reach, reach)], [c])
+        return total.reshape(2, reach, chunk, cols)
 
     def depth(src, p, x, flip):
         high, low = split(jnp.concatenate([zr[p, 0, x], src[x], zr[p, 1, x]], 0))
@@ -266,11 +286,27 @@
             est_in[x].wait()
 
     current = u0
+    every = list(range(CHUNKS))
+    edge_groups, inner_groups = order()[:2], order()[2:]
+
+    def planes_of(c):
+        return slice(c * chunk, (c + 1) * chunk)
+
+    def first_inner(p, src, slots):
+        result = blur_inner(src, slots, 0)
+        for k, c in enumerate(slots):
+            v[p, reach : reach + inner, planes_of(c), :] = result[k]
+            v_send(p, c, inner_groups)
+
+    first_inner(0, u0, every)
     for p in range(ITERS):
-        for c in range(CHUNKS):
+        for c in every:
             x_wait(current, 2 * p, c)
-            v[p, :, c * chunk : (c + 1) * chunk, :] = lateral(current, 2 * p, c, 0)
-            v_send(p, c)
+            result = blur_edges(2 * p, c, 0)
+            v[p, 0:reach, planes_of(c), :] = result[0]
+            v[p, rows - reach : rows, planes_of(c), :] = result[1]
+            v_send(p, c, edge_groups)
+
         def forward(s):
             v_wait(p, s)
             for x in range(s, s + reach):
@@ -297,13 +333,23 @@
         for s in groups[2:]:
             backward(s)
         target = out if p == ITERS - 1 else u1
-        for c in range(CHUNKS):
-            at = slice(c * chunk, (c + 1) * chunk)
+        result = blur_inner(w.at[p], every, 1)
+        for c in every:
+            at = planes_of(c)
+            target[reach : reach + inner, at, :] = (
+                current[reach : reach + inner, at, :] * result[c]
+            )
+        for c in every:
+            at = planes_of(c)
             x_wait(w.at[p], 2 * p + 1, c)
-            target[:, at, :] = current[:, at, :] * lateral(w.at[p], 2 * p + 1, c, 1)
+            result = blur_edges(2 * p + 1, c, 1)
+            for k, start in enumerate(edge_groups):
+                span = slice(start, start + reach)
+                target[span, at, :] = current[span, at, :] * result[k]
             if p < ITERS - 1:
                 x_send(u1, 2 * p + 2, False, c)
                 x_send(u1, 2 * p + 2, True, c)
+                first_inner(p + 1, u1, [c])
         current = target
 
     for there, copy in sent:
@@ -340,8 +386,8 @@
             pltpu.VMEM((ITERS,) + volume, F32),
             pltpu.VMEM((2 * ITERS, 2, reach, planes, cols), F32),
             pltpu.VMEM((2 * ITERS, 2, rows, half, cols), F32),
-            pltpu.VMEM((2, rows + 2 * reach, chunk, cols), BF16),
-            pltpu.VMEM((2, rows + 2 * reach, chunk, cols), BF16),
+            pltpu.VMEM((CHUNKS, rows + 2 * reach, chunk, cols), BF16),
+            pltpu.VMEM((CHUNKS, rows + 2 * reach, chunk, cols), BF16),
             pltpu.VMEM((2, taps, 3 * cols, cols), BF16),
             pltpu.VMEM((2, 2 * planes, 2 * (planes + 2 * half)), BF16),
             pltpu.SMEM(lateral_psf.shape, F32),

time: 81 us -> 72.9 us (0.900)
  Pallas kernels: 78.1 us -> 69.6 us
    pallas_call x1, Pallas kernels: 78.1 us -> 69.6 us  [body(): pl.pallas_call(functools.partial(kernel, nx, ng), out_shape=jax.ShapeDtyp...]
where the time goes in v3:
time: 72.9 us; the launch traced here: 72.5 us
  Pallas kernels  69.6 us (95%)
  local copies, waits for them, and re-layouts  2.81 us (4%)
    pallas_call x1, Pallas kernels, body(): pl.pallas_call(functools.partial(kernel, nx, ng), out_shape=jax.ShapeDtyp...  69.6 us
    transpose x1, local copies, waits for them, and re-layouts, body(): return jnp.swapaxes(result, 0, 1)  2.81 us

profile of v3, /device:TPU:17, one launch (start us, length us, event | category | flops | bytes accessed | tf_op | source)
XLA Modules:
  0.0 72.5 jit_solution(4514548780000685171)
XLA Ops:
  0.0 69.6 %shard_map.46 = f32[16,64,256]{2,1,0:T(8,128)} custom-call(f32[64,16,256]{2,1,0:T(8,128)} %obs_hbm.1, f32[64,16,256]{2,1,0:T(8,128)} %est_hbm.1, f32[9,9]{1,0:T(8,128)} %lat_hbm.1, f32[64]{0:T(128)} %dep_hbm.1), custom_call_target="tpu_custom_call" | custom-call | flops 14495514624 | bytes 3145728 | tf_op jit(solution)/shard_map/pallas_call | solution.py:370
  69.6 2.8 %copy.5 = f32[64,16,256]{2,1,0:T(8,128)} copy(f32[64,16,256]{2,0,1:T(8,128)} %bitcast.1) | data formatting | bytes 2097152 | tf_op jit(solution)/shard_map/transpose | solution.py:413

commit v4 on v3

--- a/solution.py
+++ b/solution.py
@@ -324,10 +324,11 @@
                     x_send(w.at[p], 2 * p + 1, s > 0, c)
 
         groups = order()
-        for s in groups[:3]:
-            forward(s)
-        for s in groups[:2]:
-            backward(s)
+        forward(groups[0])
+        forward(groups[1])
+        backward(groups[0])
+        forward(groups[2])
+        backward(groups[1])
         for s in groups[3:]:
             forward(s)
         for s in groups[2:]:

time: 72.9 us -> 72.9 us (level)
  no operation moved by 1% of the time
where the time goes in v4:
time: 72.9 us; the launch traced here: 72.5 us
  Pallas kernels  69.6 us (95%)
  local copies, waits for them, and re-layouts  2.81 us (4%)
    pallas_call x1, Pallas kernels, body(): pl.pallas_call(functools.partial(kernel, nx, ng), out_shape=jax.ShapeDtyp...  69.6 us
    transpose x1, local copies, waits for them, and re-layouts, body(): return jnp.swapaxes(result, 0, 1)  2.81 us

profile of v4, /device:TPU:17, one launch (start us, length us, event | category | flops | bytes accessed | tf_op | source)
XLA Modules:
  0.0 72.5 jit_solution(8321343540622754046)
XLA Ops:
  0.0 69.6 %shard_map.46 = f32[16,64,256]{2,1,0:T(8,128)} custom-call(f32[64,16,256]{2,1,0:T(8,128)} %obs_hbm.1, f32[64,16,256]{2,1,0:T(8,128)} %est_hbm.1, f32[9,9]{1,0:T(8,128)} %lat_hbm.1, f32[64]{0:T(128)} %dep_hbm.1), custom_call_target="tpu_custom_call" | custom-call | flops 14495514624 | bytes 3145728 | tf_op jit(solution)/shard_map/pallas_call | solution.py:371
  69.6 2.8 %copy.5 = f32[64,16,256]{2,1,0:T(8,128)} copy(f32[64,16,256]{2,0,1:T(8,128)} %bitcast.1) | data formatting | bytes 2097152 | tf_op jit(solution)/shard_map/transpose | solution.py:414
